TPU v7x, 32 devices: a whole 2x2x4 slice. The times are simulated.
32 devices in a mesh: tok: 16 (over z, x, core), voc: 2 (over y).
Axes of the slice: x: 2, y: 2, z: 4, core: 2. Of those that a mesh axis runs over, the one named last changes fastest.
Arguments:
- hidden: bfloat16 [2048, 1792], P('tok'), may hold values from -40 to 40
- head_weight: bfloat16 [1792, 16384], P(None, ('voc', 'tok')), may hold values from -0.37796447 to 0.37796447
- teacher_probs: bfloat16 [2048, 16384], P('tok', 'voc'), may hold values from 0 to 1, as said below
- teacher_row: int32 [2048], replicated, may hold values from 0 to 2047, each once
- lengths: int32 [16], replicated, may hold values from 1 to 128, as said below
Outputs:
- head_grad: bfloat16 [1792, 16384], P(None, ('voc', 'tok'))
Inputs may be any that keep to these rules, and one draw needn't show every extreme that they name: `teacher_row`: a permutation of the 2048 token positions. `lengths`: the last sequence is full. `teacher_probs`: each row is a probability distribution over the vocabulary: its entries sum to 1 up to rounding.
All inputs are finite; a program needn't handle non-finite values.
Results may differ from a plain program's by a relative error of at most 0.008.
Values may be sent and summed in bfloat16 or wider, within the bound.
A program may use at most 128 MiB of HBM per device.

v0:
```python
import jax
import jax.numpy as jnp
from jax import lax
from jax.sharding import PartitionSpec as P

SEQ_LEN = 128


loss_scale = 1048576.0


def per_device(hidden, head_weight, teacher_probs, teacher_row, lengths):
    gathered = lax.all_gather(hidden, "tok", axis=0, tiled=True)
    logits = jnp.dot(gathered, head_weight, preferred_element_type=jnp.float32)
    teacher = lax.all_to_all(teacher_probs, "tok", split_axis=1, concat_axis=0, tiled=True)
    aligned = jnp.take(teacher, teacher_row, axis=0).astype(jnp.float32)
    local_peak = jnp.max(logits, axis=1)
    row_peak = lax.pmax(local_peak, ("tok", "voc"))
    row_total = lax.psum(jnp.sum(jnp.exp(logits - row_peak[:, None]), axis=1), ("tok", "voc"))
    log_student = logits - row_peak[:, None] - jnp.log(row_total)[:, None]
    student = jnp.exp(log_student)
    log_mix = jnp.log(0.5 * aligned + 0.5 * student)
    grad_prob = 0.5 * (log_student - log_mix)
    centre = lax.psum(jnp.sum(student * grad_prob, axis=1), ("tok", "voc"))
    rows_all = logits.shape[0]
    positions = jnp.arange(rows_all, dtype=jnp.int32)
    limits = jnp.repeat(lengths, SEQ_LEN, total_repeat_length=rows_all)
    valid_mask = (positions % SEQ_LEN < limits).astype(jnp.float32)
    token_count = jnp.sum(lengths).astype(jnp.float32)
    grad_scale = loss_scale / token_count
    dlogits = ((grad_scale * valid_mask)[:, None] * student * (grad_prob - centre[:, None])).astype(
        jnp.bfloat16
    )
    head_grad = lax.dot_general(
        gathered, dlogits, (((0,), (0,)), ((), ())), preferred_element_type=jnp.float32
    )
    return head_grad.astype(jnp.bfloat16)


def solution(mesh):
    return jax.shard_map(
        per_device,
        mesh=mesh,
        in_specs=(P("tok", None), P(None, ("voc", "tok")), P("tok", "voc"), P(), P()),
        out_specs=P(None, ("voc", "tok")),
        check_vma=False,
    )
```

profile of v0, /device:TPU:0, one launch (start us, length us, event | category | flops | bytes accessed | tf_op | source)
XLA Modules:
  0.0 271.2 jit_solution(8507974441896449130)
XLA Ops:
  6.5 0.0 copy-start
  6.5 0.0 all-gather.2.cloned.1.call-start
  6.5 0.7 all-gather.2.cloned.1.call-update
  7.3 0.0 copy-start.1
  7.3 0.0 copy-start.2
  7.3 3.1 %copy.11 = bf16[16,16,8,512]{3,2,0,1:T(8,128)(2,1)} copy(bf16[16,16,8,512]{3,2,1,0:T(8,128)(2,1)} %bitcast.44) | data formatting | bytes 4194304 | tf_op jit(solution)/shard_map/all_to_all | solution.py:15
  10.4 7.4 %all-to-all-start = ((bf16[128,16,512]{2,0,1:T(8,128)(2,1)}), bf16[128,16,512]{2,0,1:T(8,128)(2,1)}, u32[]{:S(2)}, u32[]{:S(2)}) async-start(bf16[128,16,512]{2,0,1:T(8,128)(2,1)} %bitcast.43), calls=%async_computation | async-start | bytes 4194304 | tf_op jit(solution)/shard_map/all_to_all | solution.py:15
  17.8 0.0 copy-done.1
  17.8 0.6 reduce_sum.27
  19.2 0.7 fusion.17
  19.9 4.4 %compare_select_fusion.1 = (s32[2048,1]{0,1:T(1,128)S(1)}, s32[2048,1]{0,1:T(1,128)S(1)}) fusion(s32[]{:T(128)} %bitcast.13, s32[]{:T(128)} %bitcast.14, s32[]{:T(128)} %bitcast.15, s32[]{:T(128)} %bitcast.16, s32[]{:T(128)} %bitcast.17, s32[]{:T(128)} %bitcast.19, s32[]{:T(128)} %bitcast.18, s32[2048,1]{0,1:T(1,128)S(1)} %bitcast.47, s32[2048,1]{0,1:T(1,128)S(1)} %bitcast.46), kind=kLoop, calls=%fused_computation.26 | loop fusion | flops 28672 | bytes 32796 | tf_op jit(solution)/shard_map/jit(_take)/gather | solution.py:27
  24.3 0.2 compare_reduce_fusion.8
  24.6 0.0 copy-done.2
  24.6 5.6 %fusion.13 = f32[2048]{0:T(1024)S(1)} fusion(pred[2048]{0:T(1024)(128)(4,1)S(1)} %get-tuple-element.25, pred[2048]{0:T(1024)(128)(4,1)S(1)} %get-tuple-element.24, pred[2048]{0:T(1024)(128)(4,1)S(1)} %get-tuple-element.23, pred[2048]{0:T(1024)(128)(4,1)S(1)} %get-tuple-element.22, pred[2048]{0:T(1024)(128)(4,1)S(1)} %get-tuple-element.21, ...), kind=kLoop, calls=%fused_computation.45 | loop fusion | flops 53248 | bytes 34856 | tf_op jit(solution)/shard_map/mul | solution.py:31
  30.2 43.5 %all-to-all-done = bf16[128,16,512]{2,0,1:T(8,128)(2,1)} async-done(((bf16[128,16,512]{2,0,1:T(8,128)(2,1)}), bf16[128,16,512]{2,0,1:T(8,128)(2,1)}, u32[]{:S(2)}, u32[]{:S(2)}) %all-to-all-start) | async-done | bytes 2097184 | tf_op jit(solution)/shard_map/all_to_all | solution.py:15
  73.7 11.3 %gather_fusion = bf16[2048,512]{1,0:T(8,128)(2,1)} fusion(bf16[2048,512]{1,0:T(8,128)(2,1)} %bitcast.22, s32[2048]{0:T(1024)S(1)} %fusion.14), kind=kCustom, calls=%fused_computation | custom fusion | bytes 4202496 | tf_op jit(solution)/shard_map/jit(_take)/gather | solution.py:16
  85.0 3.9 %copy.7 = bf16[2048,512]{0,1:T(8,128)(2,1)} copy(bf16[2048,512]{1,0:T(8,128)(2,1)} %gather_fusion) | data formatting | bytes 4194304 | tf_op jit(solution)/shard_map/jit(_take)/gather | solution.py:16
  88.9 24.9 %all-gather.2.cloned.1.call-done = bf16[2048,1792]{1,0:T(8,128)(2,1)} async-done(((bf16[128,1792]{1,0:T(8,128)(2,1)}), bf16[2048,1792]{1,0:T(8,128)(2,1)}) %all-gather.2.cloned.1.call-update) | async-done | bytes 7340048 | tf_op jit(solution)/shard_map/all_gather | solution.py:13
  113.9 0.0 copy-done
  113.9 8.6 %fusion.18 = (f32[2048]{0:T(1024)S(1)}, f32[2048,512]{0,1:T(8,128)}) fusion(bf16[2048,1792]{1,0:T(8,128)(2,1)} %all-gather.2.cloned.1.call-done, bf16[1792,512]{1,0:T(8,128)(2,1)S(1)} %copy-done), kind=kOutput, calls=%fused_computation.50 | convolution fusion | flops 3759142912 | bytes 13377536 | tf_op jit(solution)/shard_map/dot_general | solution.py:14
  122.5 38.5 %pmax.7 = f32[2048]{0:T(1024)S(1)} all-reduce(f32[2048]{0:T(1024)S(1)} %get-tuple-element.44), channel_id=1, replica_groups=mesh['tok'=16,'voc'=2] {'tok','voc'}, use_global_device_ids=true, to_apply=%region_2.3 | all-reduce | flops 2048 | bytes 16384 | tf_op jit(solution)/shard_map/pmax | solution.py:18
  161.0 2.8 %exponential_reduce_fusion = f32[2048]{0:T(1024)S(1)} fusion(f32[2048,512]{0,1:T(8,128)} %get-tuple-element.45, f32[2048]{0:T(1024)S(1)} %pmax.7), kind=kLoop, calls=%fused_computation.4 | loop fusion | flops 2095104 | bytes 4210688 | tf_op jit(solution)/shard_map/reduce_sum | solution.py:19
  163.7 40.9 %psum.14 = f32[2048]{0:T(1024)S(1)} all-reduce(f32[2048]{0:T(1024)S(1)} %exponential_reduce_fusion), channel_id=1, replica_groups=mesh['tok'=16,'voc'=2] {'tok','voc'}, use_global_device_ids=true, to_apply=%region_4.5 | all-reduce | flops 2048 | bytes 16384 | tf_op jit(solution)/shard_map/psum | solution.py:19
  204.6 4.8 %multiply_reduce_fusion = f32[2048]{0:T(1024)S(1)} fusion(f32[2048,512]{0,1:T(8,128)} %get-tuple-element.45, f32[2048]{0:T(1024)S(1)} %log.6, f32[2048]{0:T(1024)S(1)} %pmax.7, bf16[2048,512]{0,1:T(8,128)(2,1)} %copy.7, pred[2048]{0:T(1024)(128)(4,1)S(1)} %compare_and_fusion), kind=kLoop, calls=%fused_computation.2 | loop fusion | flops 10483712 | bytes 6318080 | tf_op jit(solution)/shard_map/reduce_sum | solution.py:24
  209.4 39.4 %psum.15 = f32[2048]{0:T(1024)S(1)} all-reduce(f32[2048]{0:T(1024)S(1)} %multiply_reduce_fusion), channel_id=1, replica_groups=mesh['tok'=16,'voc'=2] {'tok','voc'}, use_global_device_ids=true, to_apply=%region_6.7 | all-reduce | flops 2048 | bytes 16384 | tf_op jit(solution)/shard_map/psum | solution.py:24
  248.9 11.7 %fusion = bf16[1792,512]{0,1:T(8,128)(2,1)} fusion(bf16[2048,1792]{1,0:T(8,128)(2,1)} %all-gather.2.cloned.1.call-done, f32[2048,512]{0,1:T(8,128)} %get-tuple-element.45, f32[2048]{0:T(1024)S(1)} %psum.15, f32[2048]{0:T(1024)S(1)} %log.6, f32[2048]{0:T(1024)S(1)} %pmax.7, f32[2048]{0:T(1024)S(1)} %fusion.13, bf16[2048,512]{0,1:T(8,128)(2,1)} %copy.7, ...), kind=kOutput, calls=%fused_computation.7 | convolution fusion | flops 3771596800 | bytes 15501312 | tf_op jit(solution)/shard_map/dot_general | solution.py:34
  260.6 3.8 %copy.8 = bf16[1792,512]{1,0:T(8,128)(2,1)} copy(bf16[1792,512]{0,1:T(8,128)(2,1)} %fusion) | data formatting | bytes 3670016 | tf_op jit(solution)/shard_map/convert_element_type | solution.py:37
  (5 shorter events, 0.0 us)
Async XLA Ops:
  6.5 107.3 %copy-start = (bf16[1792,512]{1,0:T(8,128)(2,1)S(1)}, bf16[1792,512]{1,0:T(8,128)(2,1)}, u32[]{:S(2)}) copy-start(bf16[1792,512]{1,0:T(8,128)(2,1)} %param.8) | copy-start | bytes 5505028
  6.5 107.3 %all-gather.2.cloned.1.call-start = ((), (), s32[]{:S(2)}) async-start(), calls=%async_computation.1 | async-start | bytes 7798784 | tf_op jit(solution)/shard_map/all_gather | solution.py:13
  7.3 10.6 %copy-start.1 = (s32[16]{0:T(128)S(1)}, s32[16]{0:T(128)}, u32[]{:S(2)}) copy-start(s32[16]{0:T(128)} %param.11) | copy-start | bytes 196
  7.3 17.3 %copy-start.2 = (s32[2048]{0:T(1024)S(1)}, s32[2048]{0:T(1024)}, u32[]{:S(2)}) copy-start(s32[2048]{0:T(1024)} %param.10) | copy-start | bytes 24580
  10.4 63.3 %all-to-all-start = ((bf16[128,16,512]{2,0,1:T(8,128)(2,1)}), bf16[128,16,512]{2,0,1:T(8,128)(2,1)}, u32[]{:S(2)}, u32[]{:S(2)}) async-start(bf16[128,16,512]{2,0,1:T(8,128)(2,1)} %bitcast.43), calls=%async_computation | async-start | bytes 4194304 | tf_op jit(solution)/shard_map/all_to_all | solution.py:15
Sparse Core Ops, SparseCore 0:
  9.6 104.1 all-gather.1
where the time goes:
time: 272 us; the launch traced here: 271 us
  blocking collectives  119 us (44%)
  waiting for transfers between devices  69.1 us (25%)
  local copies, waits for them, and re-layouts  23 us (8%)
  matrix products  20.3 us (7%)
  other arithmetic  18.5 us (7%)
  between operations  14.2 us (5%)
  starting transfers between devices  7.41 us (3%)
    all_to_all x1, waiting for transfers between devices, per_device(): lax.all_to_all(teacher_probs, 'tok', split_axis=1, concat_axis=0, tiled=T...  43.5 us
    psum x1, blocking collectives, per_device(): lax.psum(jnp.sum(jnp.exp(logits - row_peak[:, None]), axis=1), ('tok', 'v...  40.9 us
    psum x1, blocking collectives, per_device(): centre = lax.psum(jnp.sum(student * grad_prob, axis=1), ('tok', 'voc'))  39.4 us
    pmax x1, blocking collectives, per_device(): row_peak = lax.pmax(local_peak, ('tok', 'voc'))  38.5 us
    all_gather x1, waiting for transfers between devices, per_device(): gathered = lax.all_gather(hidden, 'tok', axis=0, tiled=True)  24.9 us
    gather x2, local copies, waits for them, and re-layouts, per_device(): aligned = jnp.take(teacher, teacher_row, axis=0).astype(jnp.float32)  15.2 us
    dot_general x1, matrix products, per_device(): lax.dot_general(gathered, dlogits, (((0,), (0,)), ((), ())), preferred_el...  11.7 us
    dot_general x1, matrix products, per_device(): logits = jnp.dot(gathered, head_weight, preferred_element_type=jnp.float32)  8.63 us
  transfers between devices with their start and end apart: 2, of which 2 were waited for; matrix products, arithmetic and copies ran while one was open for 11% of the time, Pallas kernels for 0%

commit v1 on v0

v1 whole, which is shorter than its diff:
```python
import functools

import jax
import jax.numpy as jnp
from jax import lax
from jax.experimental import pallas as pl
from jax.experimental.pallas import tpu as pltpu
from jax.sharding import PartitionSpec as P

SEQ_LEN = 128
loss_scale = 1048576.0
MESH = pl.DeviceIdType.MESH
F32 = jnp.float32
BF16 = jnp.bfloat16


def head_kernel(
    T, V,
    h_hbm, w_ref, t_hbm, trow_ref, gs_ref, out_ref,
    hbuf, tbuf, tt, wt, logits, student, aligned, dt, xl, xc, comb,
    loc_sem, zs, zr, xs, xr, ys, yr, cs, cr, ts, tr, ls, lr, es, er,
):
    N = T * V
    R, D = h_hbm.shape
    VS = w_ref.shape[1]
    TOK = T * R
    L = T // 4
    part = R // V
    G = R // 128
    me_t, me_v = lax.axis_index("tok"), lax.axis_index("voc")
    me = me_t * V + me_v
    k = lax.rem(me_t, 2)
    x = lax.rem(me_t // 2, 2)
    z = me_t // 4

    def block_of(zz, xx, kk):
        return (zz * 2 + xx) * 2 + kk

    own_h = pltpu.make_async_copy(h_hbm, hbuf.at[pl.ds(pl.multiple_of(me_t * R, R), R), :], loc_sem.at[0])
    own_h.start()
    own_t = pltpu.make_async_copy(
        t_hbm.at[:, pl.ds(pl.multiple_of(me_t * VS, VS), VS)],
        tbuf.at[pl.ds(pl.multiple_of(me_t * R, R), R), :], loc_sem.at[1])
    own_t.start()

    barrier = pltpu.get_barrier_semaphore()

    def greet(i, c):
        to = lax.rem(me + i, N)
        pl.semaphore_signal(barrier, inc=1, device_id=(to // V, lax.rem(to, V)), device_id_type=MESH)
        return c

    lax.fori_loop(1, N, greet, 0)
    own_h.wait()
    pl.semaphore_wait(barrier, N - 1)

    def rows(n, p):
        return hbuf.at[pl.ds(pl.multiple_of(n * R + p * part, part), part), :]

    def whole(n):
        return hbuf.at[pl.ds(pl.multiple_of(n * R, R), R), :]

    def remote(ref, s_sem, r_sem, tok, voc):
        return pltpu.make_async_remote_copy(
            src_ref=ref, dst_ref=ref, send_sem=s_sem, recv_sem=r_sem,
            device_id=(tok, voc), device_id_type=MESH)

    def z_copy(zp, up):
        to = jnp.minimum(z + 1, L - 1) if up else jnp.maximum(z - 1, 0)
        return remote(rows(block_of(zp, x, k), me_v), zs.at[zp, 0 if up else 1], zr.at[zp],
                      block_of(to, x, k), me_v)

    def x_copy(zp):
        return remote(rows(block_of(zp, x, k), me_v), xs.at[zp], xr.at[zp], block_of(z, 1 - x, k), me_v)

    def x_in(zp):
        return remote(rows(block_of(zp, 1 - x, k), me_v), xs.at[zp], xr.at[zp], block_of(z, 1 - x, k), me_v)

    def y_copy(zp, far, j):
        col = 1 - x if far else x
        return remote(rows(block_of(zp, col, k), me_v), ys.at[zp, far, j], yr.at[zp, far, j],
                      me_t, lax.rem(me_v + j, V))

    def y_in(zp, far, j):
        col = 1 - x if far else x
        return remote(rows(block_of(zp, col, k), lax.rem(me_v - j + V, V)), ys.at[zp, far, j], yr.at[zp, far, j],
                      me_t, lax.rem(me_v + j, V))

    def c_copy(zp, far):
        col = 1 - x if far else x
        return remote(whole(block_of(zp, col, k)), cs.at[zp, far], cr.at[zp, far], block_of(z, x, 1 - k), me_v)

    def c_in(zp, far):
        col = 1 - x if far else x
        return remote(whole(block_of(zp, col, 1 - k)), cs.at[zp, far], cr.at[zp, far], block_of(z, x, 1 - k), me_v)

    def t_copy(i):
        to = lax.rem(me_t + i, T)
        return pltpu.make_async_remote_copy(
            src_ref=t_hbm.at[:, pl.ds(pl.multiple_of(to * VS, VS), VS)],
            dst_ref=tbuf.at[pl.ds(pl.multiple_of(me_t * R, R), R), :],
            send_sem=ts.at[i], recv_sem=tr.at[i], device_id=(to, me_v), device_id_type=MESH)

    def t_in(i):
        frm = lax.rem(me_t - i + T, T)
        to = lax.rem(me_t + i, T)
        return pltpu.make_async_remote_copy(
            src_ref=t_hbm.at[:, pl.ds(pl.multiple_of(to * VS, VS), VS)],
            dst_ref=tbuf.at[pl.ds(pl.multiple_of(frm * R, R), R), :],
            send_sem=ts.at[i], recv_sem=tr.at[i], device_id=(to, me_v), device_id_type=MESH)

    def sources(d):
        if d == 0:
            return [(z, None, None)]
        return [(jnp.maximum(z - d, 0), z - d >= 0, True), (jnp.minimum(z + d, L - 1), z + d < L, False)]

    def under(cond, f):
        if cond is None:
            f()
        else:
            pl.when(cond)(f)

    def arrive(d):
        for zp, cond, up in sources(d):
            def f(zp=zp, up=up):
                if d > 0:
                    z_copy(zp, up).wait_recv()
                if d == 0 or up:
                    pl.when(z + 1 < L)(lambda: z_copy(zp, True).start())
                if d == 0 or not up:
                    pl.when(z > 0)(lambda: z_copy(zp, False).start())
                x_copy(zp).start()
                if d == 0:
                    c_copy(zp, 0).start()
                else:
                    for j in range(1, V):
                        y_copy(zp, 0, j).start()
            under(cond, f)

    def crossed(d):
        for zp, cond, up in sources(d):
            def f(zp=zp):
                x_in(zp).wait_recv()
                for j in range(1, V):
                    y_copy(zp, 1, j).start()
            under(cond, f)

    def gathered(d):
        for zp, cond, up in sources(d):
            def f(zp=zp):
                if d > 0:
                    for j in range(1, V):
                        y_in(zp, 0, j).wait_recv()
                    c_copy(zp, 0).start()
                for j in range(1, V):
                    y_in(zp, 1, j).wait_recv()
                c_copy(zp, 1).start()
            under(cond, f)

    arrive(0)

    def t_start(i, c):
        t_copy(i).start()
        return c

    lax.fori_loop(1, T, t_start, 0)

    wt[...] = w_ref[...].astype(F32).T.astype(BF16)

    crossed(0)
    for d in range(1, L):
        arrive(d)
        crossed(d)
        gathered(d - 1)
    gathered(L - 1)

    def c_wait(zp, c):
        c_in(zp, 0).wait_recv()
        c_in(zp, 1).wait_recv()
        return c

    lax.fori_loop(0, L, c_wait, 0)

    CH = 4 * R

    def logit_step(j, c):
        at = pl.ds(pl.multiple_of(j * CH, CH), CH)
        out = lax.dot_general(wt[...], hbuf[at, :], (((1,), (1,)), ((), ())), preferred_element_type=F32)
        logits[:, at] = out
        peak = jnp.max(out, axis=0, keepdims=True)
        lse = peak + jnp.log(jnp.sum(jnp.exp(out - peak), axis=0, keepdims=True))
        for q in range(CH // 128):
            xl[0, pl.ds(j * (CH // 128) + q, 1), :] = lse[:, q * 128:(q + 1) * 128]
        return c

    lax.fori_loop(0, L, logit_step, 0)

    def stat_copy(buf, s, r, i):
        to = lax.rem(me + i, N)
        return pltpu.make_async_remote_copy(
            src_ref=buf.at[0], dst_ref=buf.at[i], send_sem=s.at[i], recv_sem=r.at[i],
            device_id=(to // V, lax.rem(to, V)), device_id_type=MESH)

    def stat_start(buf, s, r):
        def go(i, c):
            stat_copy(buf, s, r, i).start()
            return c
        lax.fori_loop(1, N, go, 0)

    def stat_wait(buf, s, r):
        def go(i, c):
            stat_copy(buf, s, r, i).wait_recv()
            return c
        lax.fori_loop(1, N, go, 0)

    stat_start(xl, ls, lr)

    own_t.wait()

    def transpose_block(frm):
        blk = tbuf[pl.ds(pl.multiple_of(frm * R, R), R), :]
        tt[:, pl.ds(pl.multiple_of(frm * R, R), R)] = blk.astype(F32).T.astype(BF16)

    transpose_block(me_t)

    def t_wait(i, c):
        t_in(i).wait_recv()
        transpose_block(lax.rem(me_t - i + T, T))
        return c

    lax.fori_loop(1, T, t_wait, 0)

    PC = 256

    def align_step(j, c):
        at = pl.ds(pl.multiple_of(j * PC, PC), PC)
        row = trow_ref[:, at]
        hot = jnp.where(lax.broadcasted_iota(jnp.int32, (TOK, PC), 0) == row, 1.0, 0.0).astype(BF16)
        aligned[:, at] = jnp.dot(tt[...], hot, preferred_element_type=F32).astype(BF16)
        return c

    lax.fori_loop(0, TOK // PC, align_step, 0)

    stat_wait(xl, ls, lr)
    peak = jnp.max(xl[...], axis=0)
    comb[...] = peak + jnp.log(jnp.sum(jnp.exp(xl[...] - peak[None]), axis=0))

    def student_step(j, c):
        at = pl.ds(pl.multiple_of(j * 128, 128), 128)
        log_student = logits[:, at] - comb[pl.ds(j, 1), :]
        s = jnp.exp(log_student)
        log_mix = jnp.log(0.5 * aligned[:, at].astype(F32) + 0.5 * s)
        g = 0.5 * (log_student - log_mix)
        logits[:, at] = g
        student[:, at] = s
        xc[0, pl.ds(j, 1), :] = jnp.sum(s * g, axis=0, keepdims=True)
        return c

    lax.fori_loop(0, TOK // 128, student_step, 0)
    stat_start(xc, es, er)
    stat_wait(xc, es, er)
    comb[...] = jnp.sum(xc[...], axis=0)

    def dlogit_step(j, c):
        at = pl.ds(pl.multiple_of(j * 128, 128), 128)
        d = (gs_ref[:, at] * student[:, at]) * (logits[:, at] - comb[pl.ds(j, 1), :])
        dt[:, at] = d.astype(BF16)
        return c

    lax.fori_loop(0, TOK // 128, dlogit_step, 0)

    GC = 256

    def grad_step(j, c):
        at = pl.ds(pl.multiple_of(j * GC, GC), GC)
        g = jnp.dot(dt[...], hbuf[:, at], preferred_element_type=F32)
        out_ref[at, :] = g.T.astype(BF16)
        return c

    lax.fori_loop(0, D // GC, grad_step, 0)

    def drain_stats(i, c):
        stat_copy(xl, ls, lr, i).wait_send()
        stat_copy(xc, es, er, i).wait_send()
        return c

    lax.fori_loop(1, N, drain_stats, 0)

    def drain_teacher(i, c):
        t_copy(i).wait_send()
        return c

    lax.fori_loop(1, T, drain_teacher, 0)

    def drain_hidden(zp, c):
        pl.when((z + 1 < L) & (zp <= z))(lambda: z_copy(zp, True).wait_send())
        pl.when((z > 0) & (zp >= z))(lambda: z_copy(zp, False).wait_send())
        x_copy(zp).wait_send()
        for j in range(1, V):
            y_copy(zp, 1, j).wait_send()
            pl.when(zp != z)(lambda: y_copy(zp, 0, j).wait_send())
        c_copy(zp, 0).wait_send()
        c_copy(zp, 1).wait_send()
        return c

    lax.fori_loop(0, L, drain_hidden, 0)


def per_device(T, V, hidden, head_weight, teacher_probs, teacher_row, lengths):
    R, D = hidden.shape
    VS = head_weight.shape[1]
    TOK = T * R
    N = T * V
    L = T // 4
    valid = jnp.arange(SEQ_LEN, dtype=jnp.int32)[None, :] < lengths[:, None]
    grad_scale = loss_scale / jnp.sum(lengths).astype(F32)
    gs = (grad_scale * valid.astype(F32)).reshape(1, TOK)
    vm = pl.BlockSpec(memory_space=pltpu.VMEM)
    anyspace = pl.BlockSpec(memory_space=pl.ANY)
    dma = pltpu.SemaphoreType.DMA
    return pl.pallas_call(
        functools.partial(head_kernel, T, V),
        out_shape=jax.ShapeDtypeStruct((D, VS), BF16),
        in_specs=[anyspace, vm, anyspace, vm, vm],
        out_specs=vm,
        scratch_shapes=[
            pltpu.VMEM((TOK, D), BF16),
            pltpu.VMEM((TOK, VS), BF16),
            pltpu.VMEM((VS, TOK), BF16),
            pltpu.VMEM((VS, D), BF16),
            pltpu.VMEM((VS, TOK), F32),
            pltpu.VMEM((VS, TOK), F32),
            pltpu.VMEM((VS, TOK), BF16),
            pltpu.VMEM((VS, TOK), BF16),
            pltpu.VMEM((N, TOK // 128, 128), F32),
            pltpu.VMEM((N, TOK // 128, 128), F32),
            pltpu.VMEM((TOK // 128, 128), F32),
            dma((2,)),
            dma((L, 2)), dma((L,)),
            dma((L,)), dma((L,)),
            dma((L, 2, V)), dma((L, 2, V)),
            dma((L, 2)), dma((L, 2)),
            dma((T,)), dma((T,)),
            dma((N,)), dma((N,)),
            dma((N,)), dma((N,)),
        ],
        compiler_params=pltpu.CompilerParams(
            collective_id=0, has_side_effects=True, vmem_limit_bytes=60 * 1024 * 1024
        ),
        cost_estimate=pl.CostEstimate(
            flops=6 * TOK * D * VS, bytes_accessed=4 * TOK * D, transcendentals=4 * TOK * VS
        ),
        name="head_grad",
    )(hidden, head_weight, teacher_probs, teacher_row.reshape(1, TOK), gs)


def solution(mesh):
    return jax.shard_map(
        functools.partial(per_device, mesh.shape["tok"], mesh.shape["voc"]),
        mesh=mesh,
        in_specs=(P("tok", None), P(None, ("voc", "tok")), P("tok", "voc"), P(), P()),
        out_specs=P(None, ("voc", "tok")),
        check_vma=False,
    )
```

time: 272 us -> 121 us (0.44)
  blocking collectives: 119 us -> 0 us
  Pallas kernels: 0 us -> 115 us
  waiting for transfers between devices: 69.1 us -> 0 us
  matrix products: 20.3 us -> 0 us
  local copies, waits for them, and re-layouts: 23 us -> 2.85 us
  other arithmetic: 18.5 us -> 2.62 us
  between operations: 14.2 us -> 0.7 us
  starting transfers between devices: 7.41 us -> 0 us
    pallas_call x0 -> x1, Pallas kernels: none -> 115 us  [per_device(): pl.pallas_call(functools.partial(head_kernel, T, V), out_shape=jax.ShapeD...]
    psum x2 -> x0, blocking collectives: 80.3 us -> none  [the longest x1 40.9 us: per_device(): lax.psum(jnp.sum(jnp.exp(logits - row_peak[:, None]), axis=1), ('tok', 'v...]
    all_to_all x1 -> x0, waiting for transfers between devices: 43.5 us -> none  [per_device(): lax.all_to_all(teacher_probs, 'tok', split_axis=1, concat_axis=0, tiled=T...]
    pmax x1 -> x0, blocking collectives: 38.5 us -> none  [per_device(): row_peak = lax.pmax(local_peak, ('tok', 'voc'))]
    all_gather x1 -> x0, waiting for transfers between devices: 24.9 us -> none  [per_device(): gathered = lax.all_gather(hidden, 'tok', axis=0, tiled=True)]
    dot_general x2 -> x0, matrix products: 20.3 us -> none  [the longest x1 11.7 us: per_device(): lax.dot_general(gathered, dlogits, (((0,), (0,)), ((), ())), preferred_el...]
    gather x3 -> x0, local copies, waits for them, and re-layouts: 16 us -> none  [the longest x2 15.2 us: per_device(): aligned = jnp.take(teacher, teacher_row, axis=0).astype(jnp.float32)]
    all_to_all x1 -> x0, starting transfers between devices: 7.41 us -> none  [per_device(): lax.all_to_all(teacher_probs, 'tok', split_axis=1, concat_axis=0, tiled=T...]
  transfers between devices with their start and end apart: 2 -> 0, of which waited for: 2 -> 0; matrix products, arithmetic and copies ran while one was open for 11% -> 0% of each run, Pallas kernels for 0% -> 0%
where the time goes in v1:
time: 121 us
  Pallas kernels  115 us (95%)
  local copies, waits for them, and re-layouts  2.85 us (2%)
  other arithmetic  2.62 us (2%)
    pallas_call x1, Pallas kernels, per_device(): pl.pallas_call(functools.partial(head_kernel, T, V), out_shape=jax.ShapeD...  115 us
    unnamed x1, local copies, waits for them, and re-layouts  2.85 us

profile of v1, /device:TPU:0, one launch (start us, length us, event | category | flops | bytes accessed | tf_op | source)
XLA Modules:
  0.0 121.0 jit_solution(16909770610809778306)
XLA Ops:
  0.0 1.3 %reduce_sum.9 = s32[]{:T(128)} reduce(s32[16]{0:T(128)} %param.9, s32[]{:T(128)} %constant.4.clone.1), dimensions={0}, to_apply=%region_0.0 | reduce | flops 15 | bytes 72 | tf_op jit(solution)/shard_map/reduce_sum | solution.py:316
  2.0 1.3 %fusion = f32[16,128]{1,0:T(8,128)} fusion(f32[]{:T(128)S(6)} %div.3, s32[16]{0:T(128)} %param.9), kind=kLoop, calls=%fused_computation.1 | loop fusion | flops 4096 | bytes 8260 | tf_op jit(solution)/shard_map/mul | solution.py:317
  3.3 114.8 %head_grad.1 = bf16[1792,512]{1,0:T(8,128)(2,1)} custom-call(bf16[128,1792]{1,0:T(8,128)(2,1)} %h_hbm.1, bf16[1792,512]{1,0:T(8,128)(2,1)} %w_ref.1, bf16[128,8192]{1,0:T(8,128)(2,1)} %t_hbm.1, s32[1,2048]{1,0:T(1,128)} %bitcast.3, f32[1,2048]{1,0:T(1,128)} %bitcast.2), custom_call_target="tpu_custom_call" | custom-call | flops 11274289152 | bytes 14680064 | tf_op jit(solution)/shard_map/head_grad/pallas_call | solution.py:321
  118.1 2.8 %copy.7 = bf16[1792,512]{1,0:T(8,128)(2,1)} copy(bf16[1792,512]{1,0:T(8,128)(2,1)} %head_grad.1) | data formatting | bytes 3670016

commit v2 on v1

--- a/solution.py
+++ b/solution.py
@@ -16,17 +16,16 @@
 
 def head_kernel(
     T, V,
-    h_hbm, w_ref, t_hbm, trow_ref, gs_ref, out_ref,
-    hbuf, tbuf, tt, wt, logits, student, aligned, dt, xl, xc, comb,
+    h_hbm, w_hbm, t_hbm, trow_ref, len_ref, out_ref,
+    wbuf, hot, hbuf, tbuf, tt, wt, logits, student, aligned, dt, xl, xc, comb,
     loc_sem, zs, zr, xs, xr, ys, yr, cs, cr, ts, tr, ls, lr, es, er,
 ):
     N = T * V
     R, D = h_hbm.shape
-    VS = w_ref.shape[1]
+    VS = w_hbm.shape[1]
     TOK = T * R
     L = T // 4
     part = R // V
-    G = R // 128
     me_t, me_v = lax.axis_index("tok"), lax.axis_index("voc")
     me = me_t * V + me_v
     k = lax.rem(me_t, 2)
@@ -42,6 +41,9 @@
         t_hbm.at[:, pl.ds(pl.multiple_of(me_t * VS, VS), VS)],
         tbuf.at[pl.ds(pl.multiple_of(me_t * R, R), R), :], loc_sem.at[1])
     own_t.start()
+
+    own_w = pltpu.make_async_copy(w_hbm, wbuf, loc_sem.at[2])
+    own_w.start()
 
     barrier = pltpu.get_barrier_semaphore()
 
@@ -157,22 +159,46 @@
                 c_copy(zp, 1).start()
             under(cond, f)
 
+    def t_start(i, c):
+        to_z = lax.rem(me_t + i, T) // 4
+        far = to_z != z
+        pl.when(far if c else jnp.logical_not(far))(lambda: t_copy(i).start())
+
+    def t_starts(across):
+        def go(i, c):
+            t_start(i, across)
+            return c
+        lax.fori_loop(1, T, go, 0)
+
+    HC = 256
+
+    def hot_chunk(j):
+        row = trow_ref[:, pl.ds(pl.multiple_of(j * HC, HC), HC)]
+        return jnp.where(lax.broadcasted_iota(jnp.int32, (TOK, HC), 0) == row, 1.0, 0.0).astype(BF16)
+
+    keep_hot = hot.shape[1] == TOK
+
     arrive(0)
-
-    def t_start(i, c):
-        t_copy(i).start()
-        return c
-
-    lax.fori_loop(1, T, t_start, 0)
-
-    wt[...] = w_ref[...].astype(F32).T.astype(BF16)
-
+    t_starts(False)
+    own_w.wait()
+    wt[...] = wbuf[...].astype(F32).T.astype(BF16)
+    arrive(1)
     crossed(0)
+    for d in range(2, L):
+        arrive(d)
+        crossed(d - 1)
+    t_starts(True)
+    if keep_hot:
+        def hot_step(j, c):
+            hot[:, pl.ds(pl.multiple_of(j * HC, HC), HC)] = hot_chunk(j)
+            return c
+        lax.fori_loop(0, TOK // HC // 2, hot_step, 0)
+    gathered(0)
+    crossed(L - 1)
     for d in range(1, L):
-        arrive(d)
-        crossed(d)
-        gathered(d - 1)
-    gathered(L - 1)
+        gathered(d)
+    if keep_hot:
+        lax.fori_loop(TOK // HC // 2, TOK // HC, hot_step, 0)
 
     def c_wait(zp, c):
         c_in(zp, 0).wait_recv()
@@ -230,16 +256,13 @@
 
     lax.fori_loop(1, T, t_wait, 0)
 
-    PC = 256
-
     def align_step(j, c):
-        at = pl.ds(pl.multiple_of(j * PC, PC), PC)
-        row = trow_ref[:, at]
-        hot = jnp.where(lax.broadcasted_iota(jnp.int32, (TOK, PC), 0) == row, 1.0, 0.0).astype(BF16)
-        aligned[:, at] = jnp.dot(tt[...], hot, preferred_element_type=F32).astype(BF16)
-        return c
-
-    lax.fori_loop(0, TOK // PC, align_step, 0)
+        at = pl.ds(pl.multiple_of(j * HC, HC), HC)
+        pick = hot[:, at] if keep_hot else hot_chunk(j)
+        aligned[:, at] = jnp.dot(tt[...], pick, preferred_element_type=F32).astype(BF16)
+        return c
+
+    lax.fori_loop(0, TOK // HC, align_step, 0)
 
     stat_wait(xl, ls, lr)
     peak = jnp.max(xl[...], axis=0)
@@ -261,9 +284,14 @@
     stat_wait(xc, es, er)
     comb[...] = jnp.sum(xc[...], axis=0)
 
+    count = lax.fori_loop(0, TOK // SEQ_LEN, lambda j, c: c + len_ref[j], jnp.int32(0))
+    grad_scale = loss_scale / jnp.full((1, SEQ_LEN), count, jnp.int32).astype(F32)
+    slot = lax.broadcasted_iota(jnp.int32, (1, SEQ_LEN), 1)
+
     def dlogit_step(j, c):
-        at = pl.ds(pl.multiple_of(j * 128, 128), 128)
-        d = (gs_ref[:, at] * student[:, at]) * (logits[:, at] - comb[pl.ds(j, 1), :])
+        at = pl.ds(pl.multiple_of(j * SEQ_LEN, SEQ_LEN), SEQ_LEN)
+        scale = jnp.where(slot < len_ref[j], grad_scale, 0.0)
+        d = (scale * student[:, at]) * (logits[:, at] - comb[pl.ds(j, 1), :])
         dt[:, at] = d.astype(BF16)
         return c
 
@@ -312,18 +340,17 @@
     TOK = T * R
     N = T * V
     L = T // 4
-    valid = jnp.arange(SEQ_LEN, dtype=jnp.int32)[None, :] < lengths[:, None]
-    grad_scale = loss_scale / jnp.sum(lengths).astype(F32)
-    gs = (grad_scale * valid.astype(F32)).reshape(1, TOK)
     vm = pl.BlockSpec(memory_space=pltpu.VMEM)
     anyspace = pl.BlockSpec(memory_space=pl.ANY)
     dma = pltpu.SemaphoreType.DMA
     return pl.pallas_call(
         functools.partial(head_kernel, T, V),
         out_shape=jax.ShapeDtypeStruct((D, VS), BF16),
-        in_specs=[anyspace, vm, anyspace, vm, vm],
+        in_specs=[anyspace, anyspace, anyspace, vm, pl.BlockSpec(memory_space=pltpu.SMEM)],
         out_specs=vm,
         scratch_shapes=[
+            pltpu.VMEM((D, VS), BF16),
+            pltpu.VMEM((TOK, TOK) if TOK * TOK <= 2**22 else (16, 128), BF16),
             pltpu.VMEM((TOK, D), BF16),
             pltpu.VMEM((TOK, VS), BF16),
             pltpu.VMEM((VS, TOK), BF16),
@@ -335,7 +362,7 @@
             pltpu.VMEM((N, TOK // 128, 128), F32),
             pltpu.VMEM((N, TOK // 128, 128), F32),
             pltpu.VMEM((TOK // 128, 128), F32),
-            dma((2,)),
+            dma((3,)),
             dma((L, 2)), dma((L,)),
             dma((L,)), dma((L,)),
             dma((L, 2, V)), dma((L, 2, V)),
@@ -351,7 +378,7 @@
             flops=6 * TOK * D * VS, bytes_accessed=4 * TOK * D, transcendentals=4 * TOK * VS
         ),
         name="head_grad",
-    )(hidden, head_weight, teacher_probs, teacher_row.reshape(1, TOK), gs)
+    )(hidden, head_weight, teacher_probs, teacher_row.reshape(1, TOK), lengths)
 
 
 def solution(mesh):

time: 121 us -> 120 us (level)
  other arithmetic: 2.62 us -> 0 us
  Pallas kernels: 115 us -> 117 us
    pallas_call x1, Pallas kernels: 115 us -> 117 us  [per_device(): pl.pallas_call(functools.partial(head_kernel, T, V), out_shape=jax.ShapeD...]
    mul x1 -> x0, other arithmetic: 1.33 us -> none  [per_device(): gs = (grad_scale * valid.astype(F32)).reshape(1, TOK)]
    reduce_sum x1 -> x0, other arithmetic: 1.29 us -> none  [per_device(): grad_scale = loss_scale / jnp.sum(lengths).astype(F32)]
where the time goes in v2:
time: 120 us
  Pallas kernels  117 us (98%)
  local copies, waits for them, and re-layouts  2.85 us (2%)
    pallas_call x1, Pallas kernels, per_device(): pl.pallas_call(functools.partial(head_kernel, T, V), out_shape=jax.ShapeD...  117 us
    unnamed x1, local copies, waits for them, and re-layouts  2.85 us

profile of v2, /device:TPU:0, one launch (start us, length us, event | category | flops | bytes accessed | tf_op | source)
XLA Modules:
  0.0 119.9 jit_solution(18238526751067915555)
XLA Ops:
  0.0 117.0 %head_grad.1 = bf16[1792,512]{1,0:T(8,128)(2,1)} custom-call(bf16[128,1792]{1,0:T(8,128)(2,1)} %h_hbm.1, bf16[1792,512]{1,0:T(8,128)(2,1)} %w_hbm.1, bf16[128,8192]{1,0:T(8,128)(2,1)} %t_hbm.1, s32[1,2048]{1,0:T(1,128)} %bitcast.1, s32[16]{0:T(128)} %len_ref.1), custom_call_target="tpu_custom_call" | custom-call | flops 11274289152 | bytes 14680064 | tf_op jit(solution)/shard_map/head_grad/pallas_call | solution.py:346
  117.0 2.8 %copy.7 = bf16[1792,512]{1,0:T(8,128)(2,1)} copy(bf16[1792,512]{1,0:T(8,128)(2,1)} %head_grad.1) | data formatting | bytes 3670016

commit v3 on v2

--- a/solution.py
+++ b/solution.py
@@ -17,7 +17,7 @@
 def head_kernel(
     T, V,
     h_hbm, w_hbm, t_hbm, trow_ref, len_ref, out_ref,
-    wbuf, hot, hbuf, tbuf, tt, wt, logits, student, aligned, dt, xl, xc, comb,
+    wbuf, hot, hbuf, tload, tsend, tt, wt, logits, student, dt, xl, xc, comb,
     loc_sem, zs, zr, xs, xr, ys, yr, cs, cr, ts, tr, ls, lr, es, er,
 ):
     N = T * V
@@ -37,9 +37,7 @@
 
     own_h = pltpu.make_async_copy(h_hbm, hbuf.at[pl.ds(pl.multiple_of(me_t * R, R), R), :], loc_sem.at[0])
     own_h.start()
-    own_t = pltpu.make_async_copy(
-        t_hbm.at[:, pl.ds(pl.multiple_of(me_t * VS, VS), VS)],
-        tbuf.at[pl.ds(pl.multiple_of(me_t * R, R), R), :], loc_sem.at[1])
+    own_t = pltpu.make_async_copy(t_hbm, tload, loc_sem.at[1])
     own_t.start()
 
     own_w = pltpu.make_async_copy(w_hbm, wbuf, loc_sem.at[2])
@@ -96,20 +94,15 @@
         col = 1 - x if far else x
         return remote(whole(block_of(zp, col, 1 - k)), cs.at[zp, far], cr.at[zp, far], block_of(z, x, 1 - k), me_v)
 
-    def t_copy(i):
+    def t_copy(i, frm=me_t):
         to = lax.rem(me_t + i, T)
         return pltpu.make_async_remote_copy(
-            src_ref=t_hbm.at[:, pl.ds(pl.multiple_of(to * VS, VS), VS)],
-            dst_ref=tbuf.at[pl.ds(pl.multiple_of(me_t * R, R), R), :],
+            src_ref=tsend.at[pl.ds(pl.multiple_of(to * VS, VS), VS), :],
+            dst_ref=tt.at[:, pl.ds(pl.multiple_of(frm * R, R), R)],
             send_sem=ts.at[i], recv_sem=tr.at[i], device_id=(to, me_v), device_id_type=MESH)
 
     def t_in(i):
-        frm = lax.rem(me_t - i + T, T)
-        to = lax.rem(me_t + i, T)
-        return pltpu.make_async_remote_copy(
-            src_ref=t_hbm.at[:, pl.ds(pl.multiple_of(to * VS, VS), VS)],
-            dst_ref=tbuf.at[pl.ds(pl.multiple_of(frm * R, R), R), :],
-            send_sem=ts.at[i], recv_sem=tr.at[i], device_id=(to, me_v), device_id_type=MESH)
+        return t_copy(i, lax.rem(me_t - i + T, T))
 
     def sources(d):
         if d == 0:
@@ -178,8 +171,17 @@
 
     keep_hot = hot.shape[1] == TOK
 
+    def turn_step(j, c):
+        at = pl.ds(pl.multiple_of(j * VS, VS), VS)
+        tsend[at, :] = tload[:, at].astype(F32).T.astype(BF16)
+        return c
+
     arrive(0)
+    own_t.wait()
+    lax.fori_loop(0, T, turn_step, 0)
     t_starts(False)
+    mine = pl.ds(pl.multiple_of(me_t * R, R), R)
+    tt[:, mine] = tsend[pl.ds(pl.multiple_of(me_t * VS, VS), VS), :]
     own_w.wait()
     wt[...] = wbuf[...].astype(F32).T.astype(BF16)
     arrive(1)
@@ -241,45 +243,30 @@
 
     stat_start(xl, ls, lr)
 
-    own_t.wait()
-
-    def transpose_block(frm):
-        blk = tbuf[pl.ds(pl.multiple_of(frm * R, R), R), :]
-        tt[:, pl.ds(pl.multiple_of(frm * R, R), R)] = blk.astype(F32).T.astype(BF16)
-
-    transpose_block(me_t)
-
     def t_wait(i, c):
         t_in(i).wait_recv()
-        transpose_block(lax.rem(me_t - i + T, T))
         return c
 
     lax.fori_loop(1, T, t_wait, 0)
-
-    def align_step(j, c):
-        at = pl.ds(pl.multiple_of(j * HC, HC), HC)
-        pick = hot[:, at] if keep_hot else hot_chunk(j)
-        aligned[:, at] = jnp.dot(tt[...], pick, preferred_element_type=F32).astype(BF16)
-        return c
-
-    lax.fori_loop(0, TOK // HC, align_step, 0)
 
     stat_wait(xl, ls, lr)
     peak = jnp.max(xl[...], axis=0)
     comb[...] = peak + jnp.log(jnp.sum(jnp.exp(xl[...] - peak[None]), axis=0))
 
-    def student_step(j, c):
-        at = pl.ds(pl.multiple_of(j * 128, 128), 128)
-        log_student = logits[:, at] - comb[pl.ds(j, 1), :]
-        s = jnp.exp(log_student)
-        log_mix = jnp.log(0.5 * aligned[:, at].astype(F32) + 0.5 * s)
-        g = 0.5 * (log_student - log_mix)
-        logits[:, at] = g
-        student[:, at] = s
-        xc[0, pl.ds(j, 1), :] = jnp.sum(s * g, axis=0, keepdims=True)
-        return c
-
-    lax.fori_loop(0, TOK // 128, student_step, 0)
+    for j in range(TOK // HC):
+        pick = hot[:, j * HC:(j + 1) * HC] if keep_hot else hot_chunk(j)
+        aligned = jnp.dot(tt[...], pick, preferred_element_type=F32)
+        for q in range(HC // 128):
+            row = j * (HC // 128) + q
+            at = slice(row * 128, (row + 1) * 128)
+            log_student = logits[:, at] - comb[row:row + 1, :]
+            s = jnp.exp(log_student)
+            log_mix = jnp.log(0.5 * aligned[:, q * 128:(q + 1) * 128] + 0.5 * s)
+            g = 0.5 * (log_student - log_mix)
+            logits[:, at] = g
+            student[:, at] = s
+            xc[0, row:row + 1, :] = jnp.sum(s * g, axis=0, keepdims=True)
+
     stat_start(xc, es, er)
     stat_wait(xc, es, er)
     comb[...] = jnp.sum(xc[...], axis=0)
@@ -299,13 +286,10 @@
 
     GC = 256
 
-    def grad_step(j, c):
-        at = pl.ds(pl.multiple_of(j * GC, GC), GC)
+    for j in range(D // GC):
+        at = slice(j * GC, (j + 1) * GC)
         g = jnp.dot(dt[...], hbuf[:, at], preferred_element_type=F32)
         out_ref[at, :] = g.T.astype(BF16)
-        return c
-
-    lax.fori_loop(0, D // GC, grad_step, 0)
 
     def drain_stats(i, c):
         stat_copy(xl, ls, lr, i).wait_send()
@@ -352,12 +336,12 @@
             pltpu.VMEM((D, VS), BF16),
             pltpu.VMEM((TOK, TOK) if TOK * TOK <= 2**22 else (16, 128), BF16),
             pltpu.VMEM((TOK, D), BF16),
-            pltpu.VMEM((TOK, VS), BF16),
+            pltpu.VMEM((R, T * VS), BF16),
+            pltpu.VMEM((T * VS, R), BF16),
             pltpu.VMEM((VS, TOK), BF16),
             pltpu.VMEM((VS, D), BF16),
             pltpu.VMEM((VS, TOK), F32),
             pltpu.VMEM((VS, TOK), F32),
-            pltpu.VMEM((VS, TOK), BF16),
             pltpu.VMEM((VS, TOK), BF16),
             pltpu.VMEM((N, TOK // 128, 128), F32),
             pltpu.VMEM((N, TOK // 128, 128), F32),

time: 120 us -> 120 us (level)
  no operation moved by 1% of the time
where the time goes in v3:
time: 120 us
  Pallas kernels  117 us (98%)
  local copies, waits for them, and re-layouts  2.85 us (2%)
    pallas_call x1, Pallas kernels, per_device(): pl.pallas_call(functools.partial(head_kernel, T, V), out_shape=jax.ShapeD...  117 us
    unnamed x1, local copies, waits for them, and re-layouts  2.85 us

profile of v3, /device:TPU:0, one launch (start us, length us, event | category | flops | bytes accessed | tf_op | source)
XLA Modules:
  0.0 119.6 jit_solution(3024354396246353677)
XLA Ops:
  0.0 116.8 %head_grad.1 = bf16[1792,512]{1,0:T(8,128)(2,1)} custom-call(bf16[128,1792]{1,0:T(8,128)(2,1)} %h_hbm.1, bf16[1792,512]{1,0:T(8,128)(2,1)} %w_hbm.1, bf16[128,8192]{1,0:T(8,128)(2,1)} %t_hbm.1, s32[1,2048]{1,0:T(1,128)} %bitcast.1, s32[16]{0:T(128)} %len_ref.1), custom_call_target="tpu_custom_call" | custom-call | flops 11274289152 | bytes 14680064 | tf_op jit(solution)/shard_map/head_grad/pallas_call | solution.py:330
  116.8 2.8 %copy.7 = bf16[1792,512]{1,0:T(8,128)(2,1)} copy(bf16[1792,512]{1,0:T(8,128)(2,1)} %head_grad.1) | data formatting | bytes 3670016

commit v4 on v3

--- a/solution.py
+++ b/solution.py
@@ -177,30 +177,32 @@
         return c
 
     arrive(0)
-    own_t.wait()
-    lax.fori_loop(0, T, turn_step, 0)
-    t_starts(False)
-    mine = pl.ds(pl.multiple_of(me_t * R, R), R)
-    tt[:, mine] = tsend[pl.ds(pl.multiple_of(me_t * VS, VS), VS), :]
     own_w.wait()
     wt[...] = wbuf[...].astype(F32).T.astype(BF16)
     arrive(1)
+    own_t.wait()
+    lax.fori_loop(0, T, turn_step, 0)
+    t_starts(True)
+    t_starts(False)
     crossed(0)
     for d in range(2, L):
         arrive(d)
         crossed(d - 1)
-    t_starts(True)
+        gathered(d - 2)
+    mine = pl.ds(pl.multiple_of(me_t * R, R), R)
+    tt[:, mine] = tsend[pl.ds(pl.multiple_of(me_t * VS, VS), VS), :]
     if keep_hot:
         def hot_step(j, c):
             hot[:, pl.ds(pl.multiple_of(j * HC, HC), HC)] = hot_chunk(j)
             return c
         lax.fori_loop(0, TOK // HC // 2, hot_step, 0)
-    gathered(0)
     crossed(L - 1)
-    for d in range(1, L):
-        gathered(d)
+    gathered(L - 2)
     if keep_hot:
         lax.fori_loop(TOK // HC // 2, TOK // HC, hot_step, 0)
+    gathered(L - 1)
+
+    CH = 4 * R
 
     def c_wait(zp, c):
         c_in(zp, 0).wait_recv()
@@ -209,16 +211,15 @@
 
     lax.fori_loop(0, L, c_wait, 0)
 
-    CH = 4 * R
-
-    def logit_step(j, c):
-        at = pl.ds(pl.multiple_of(j * CH, CH), CH)
+    def logit_step(zp, c):
+        at = pl.ds(pl.multiple_of(zp * CH, CH), CH)
         out = lax.dot_general(wt[...], hbuf[at, :], (((1,), (1,)), ((), ())), preferred_element_type=F32)
         logits[:, at] = out
         peak = jnp.max(out, axis=0, keepdims=True)
         lse = peak + jnp.log(jnp.sum(jnp.exp(out - peak), axis=0, keepdims=True))
         for q in range(CH // 128):
-            xl[0, pl.ds(j * (CH // 128) + q, 1), :] = lse[:, q * 128:(q + 1) * 128]
+            xl[0, pl.ds(zp * (CH // 128) + q, 1), :] = lse[:, q * 128:(q + 1) * 128]
+
         return c
 
     lax.fori_loop(0, L, logit_step, 0)

time: 120 us -> 116 us (0.967)
  Pallas kernels: 117 us -> 113 us
    pallas_call x1, Pallas kernels: 117 us -> 113 us  [per_device(): pl.pallas_call(functools.partial(head_kernel, T, V), out_shape=jax.ShapeD...]
where the time goes in v4:
time: 116 us
  Pallas kernels  113 us (97%)
  local copies, waits for them, and re-layouts  2.85 us (2%)
    pallas_call x1, Pallas kernels, per_device(): pl.pallas_call(functools.partial(head_kernel, T, V), out_shape=jax.ShapeD...  113 us
    unnamed x1, local copies, waits for them, and re-layouts  2.85 us

profile of v4, /device:TPU:0, one launch (start us, length us, event | category | flops | bytes accessed | tf_op | source)
XLA Modules:
  0.0 115.8 jit_solution(11840704111999737482)
XLA Ops:
  0.0 112.9 %head_grad.1 = bf16[1792,512]{1,0:T(8,128)(2,1)} custom-call(bf16[128,1792]{1,0:T(8,128)(2,1)} %h_hbm.1, bf16[1792,512]{1,0:T(8,128)(2,1)} %w_hbm.1, bf16[128,8192]{1,0:T(8,128)(2,1)} %t_hbm.1, s32[1,2048]{1,0:T(1,128)} %bitcast.1, s32[16]{0:T(128)} %len_ref.1), custom_call_target="tpu_custom_call" | custom-call | flops 11274289152 | bytes 14680064 | tf_op jit(solution)/shard_map/head_grad/pallas_call | solution.py:331
  112.9 2.8 %copy.7 = bf16[1792,512]{1,0:T(8,128)(2,1)} copy(bf16[1792,512]{1,0:T(8,128)(2,1)} %head_grad.1) | data formatting | bytes 3670016

commit v5 on v4

--- a/solution.py
+++ b/solution.py
@@ -177,8 +177,6 @@
         return c
 
     arrive(0)
-    own_w.wait()
-    wt[...] = wbuf[...].astype(F32).T.astype(BF16)
     arrive(1)
     own_t.wait()
     lax.fori_loop(0, T, turn_step, 0)
@@ -189,6 +187,8 @@
         arrive(d)
         crossed(d - 1)
         gathered(d - 2)
+    own_w.wait()
+    wt[...] = wbuf[...].astype(F32).T.astype(BF16)
     mine = pl.ds(pl.multiple_of(me_t * R, R), R)
     tt[:, mine] = tsend[pl.ds(pl.multiple_of(me_t * VS, VS), VS), :]
     if keep_hot:

time: 116 us -> 116 us (level)
  no operation moved by 1% of the time
where the time goes in v5:
time: 116 us
  Pallas kernels  113 us (97%)
  local copies, waits for them, and re-layouts  2.85 us (2%)
    pallas_call x1, Pallas kernels, per_device(): pl.pallas_call(functools.partial(head_kernel, T, V), out_shape=jax.ShapeD...  113 us
    unnamed x1, local copies, waits for them, and re-layouts  2.85 us

profile of v5, /device:TPU:0, one launch (start us, length us, event | category | flops | bytes accessed | tf_op | source)
XLA Modules:
  0.0 115.8 jit_solution(11502358715918963286)
XLA Ops:
  0.0 112.9 %head_grad.1 = bf16[1792,512]{1,0:T(8,128)(2,1)} custom-call(bf16[128,1792]{1,0:T(8,128)(2,1)} %h_hbm.1, bf16[1792,512]{1,0:T(8,128)(2,1)} %w_hbm.1, bf16[128,8192]{1,0:T(8,128)(2,1)} %t_hbm.1, s32[1,2048]{1,0:T(1,128)} %bitcast.1, s32[16]{0:T(128)} %len_ref.1), custom_call_target="tpu_custom_call" | custom-call | flops 11274289152 | bytes 14680064 | tf_op jit(solution)/shard_map/head_grad/pallas_call | solution.py:331
  112.9 2.8 %copy.7 = bf16[1792,512]{1,0:T(8,128)(2,1)} copy(bf16[1792,512]{1,0:T(8,128)(2,1)} %head_grad.1) | data formatting | bytes 3670016
